TPU v7x, 32 devices: a whole 2x2x4 slice. The times are simulated.
32 devices in a mesh: groups: 2 (over y), blk: 4 (over z), cells: 2 (over x), rep: 2 (over core).
Axes of the slice: x: 2, y: 2, z: 4, core: 2. Of those that a mesh axis runs over, the one named last changes fastest.
Arguments:
- probes: bfloat16 [32, 2, 4096], P('rep', 'cells', ('groups', 'blk')), parts along dimension 2, may hold values from -6 to 6
- depth_level: int32 [2, 4096], P('cells', ('groups', 'blk')), parts along dimension 1, may hold values from 0 to 15
- depth_scale: float32 [16], replicated, may hold values from 0.2 to 1.5
- sensitivity: bfloat16 [6, 3072, 2, 2048], P(None, ('groups', 'blk'), 'cells'), parts along dimension 1, may hold values from -0.125 to 0.125
- data_weight: float32 [6, 3072], P(None, ('groups', 'blk')), parts along dimension 1, may hold values from 0.05 to 0.5
- face_first: int32 [2, 2048], P('cells', ('groups', 'blk')), parts along dimension 1, may hold values from 0 to 2047, as said below
- face_second: int32 [2, 2048], P('cells', ('groups', 'blk')), parts along dimension 1, may hold values from 0 to 4095, as said below
- face_coef: float32 [2, 2048], P('cells', ('groups', 'blk')), parts along dimension 1, may hold values from 0.2 to 0.8
- face_count: int32 [2, 8], P('cells', ('groups', 'blk')), parts along dimension 1, may hold values from 51 to 256, as said below
Outputs:
- hessian_probe: float32 [32, 2, 4096], P('rep', 'cells', ('groups', 'blk')), parts along dimension 2
There are 2 independent parts, one for each index of `groups`. A program takes and returns all parts, laid end to end along the dimension named above; an argument that names none is the same for every part. Nothing has to cross between parts.
Inputs may be any that keep to these rules, and one draw needn't show every extreme that they name: `face_first`: a cell number within partition p. `face_second`: never equal to face_first of the same slot; values of 2048 or more name cells of the next partition, which the last partition never does. Only the first face_count[p, b] slots of block b of partition p (slots b * 256 onward) hold faces, the others are ignored; in every draw some block is full.
All inputs are finite; a program needn't handle non-finite values.
Results may differ from a plain program's by a relative error of at most 0.0029.
Values may be sent and summed in bfloat16 or wider, within the bound.
A program may use at most 64 MiB of HBM per device.

v0:
```python
import jax
import jax.numpy as jnp
from jax import lax
from jax.sharding import PartitionSpec as P


def shifted(block, axis, distance):
    devices = range(lax.axis_size(axis))
    route = [(i - distance, i) for i in devices if i - distance in devices]
    return lax.ppermute(block, axis, route)


def level_scale(depth_level, depth_scale):
    levels = jnp.arange(depth_scale.shape[0], dtype=jnp.int32)
    pick_rows = (depth_level[..., None] == levels).astype(jnp.float32)
    return jnp.sum(pick_rows * depth_scale, axis=-1)


def pick_hot(indices, offset, count):
    return (indices[:, None] - offset == jnp.arange(count, dtype=jnp.int32)[None, :]).astype(
        jnp.bfloat16
    )


def pick_values(block, hot):
    dims = (((1,), (1,)), ((), ()))
    return lax.dot_general(block, hot, dims, preferred_element_type=jnp.float32)


def spread_flux(flux, hot):
    upper = flux.astype(jnp.bfloat16)
    lower = (flux - upper.astype(jnp.float32)).astype(jnp.bfloat16)
    return jnp.dot(upper, hot, preferred_element_type=jnp.float32) + jnp.dot(
        lower, hot, preferred_element_type=jnp.float32
    )


def on_device(
    probes,
    depth_level,
    depth_scale,
    sensitivity,
    data_weight,
    face_first,
    face_second,
    face_coef,
    face_count,
):
    own_scale = level_scale(depth_level, depth_scale)
    weighted = (probes.astype(jnp.float32) * own_scale[None]).astype(jnp.bfloat16)
    probe_block = lax.all_gather(weighted, "blk", axis=2, tiled=True)
    slot_count = face_first.shape[1]
    live_all = (jnp.arange(slot_count, dtype=jnp.int32) < face_count[0, 0]).astype(jnp.float32)
    matrix = sensitivity[:, :, 0, :]
    first_cell = face_first[0]
    second_cell = face_second[0]
    coef_slots = face_coef[0]
    probe_cols = probe_block[:, 0, :]
    part_cells = probe_cols.shape[1]
    partial_value = jnp.einsum(
        "msc,qc->qms", matrix, probe_cols, preferred_element_type=jnp.float32
    )
    predicted = lax.psum(partial_value, "cells")
    residual = (data_weight[None] * predicted).astype(jnp.bfloat16)
    adjoint = jnp.einsum("msc,qms->qc", matrix, residual, preferred_element_type=jnp.float32)
    first_hot = pick_hot(first_cell, 0, part_cells)
    second_own = pick_hot(second_cell, 0, part_cells)
    first_val = pick_values(probe_cols, first_hot)
    second_val = pick_values(probe_cols, second_own)
    crossing = (second_cell >= part_cells).astype(jnp.float32)
    asked = shifted(second_cell, "cells", 1)
    asked_hot = pick_hot(asked, part_cells, part_cells)
    answer = pick_values(probe_cols, asked_hot).astype(jnp.bfloat16)
    received = shifted(answer, "cells", -1)
    second_val = second_val + crossing * received.astype(jnp.float32)
    flux_term = coef_slots * (coef_slots * live_all * (first_val - second_val))
    own_term = spread_flux(flux_term, first_hot) - spread_flux(flux_term, second_own)
    sent_flux = shifted(flux_term * crossing, "cells", 1)
    arrived = -spread_flux(sent_flux, asked_hot)
    total_term = (adjoint + own_term + arrived)[:, None, :]
    result = lax.psum_scatter(total_term, "blk", scatter_dimension=2, tiled=True)
    return result * own_scale[None]


def solution(mesh):
    return jax.shard_map(
        on_device,
        mesh=mesh,
        in_specs=(
            P("rep", "cells", ("groups", "blk")),
            P("cells", ("groups", "blk")),
            P(),
            P(None, ("groups", "blk"), "cells", None),
            P(None, ("groups", "blk")),
            P("cells", ("groups", "blk")),
            P("cells", ("groups", "blk")),
            P("cells", ("groups", "blk")),
            P("cells", ("groups", "blk")),
        ),
        out_specs=P("rep", "cells", ("groups", "blk")),
        check_vma=False,
    )
```

profile of v0, /device:TPU:0, one launch (start us, length us, event | category | flops | bytes accessed | tf_op | source)
XLA Modules:
  0.0 87.3 jit_solution(1859797593118502068)
XLA Ops:
  6.5 0.0 all-reduce.2.cloned.1.call-start
  6.5 0.8 select_reduce_fusion
  7.3 0.7 multiply_convert_fusion.2
  8.0 14.9 %all_gather.3 = bf16[16,1,2048]{2,0,1:T(8,128)(2,1)S(1)} all-gather(bf16[16,1,512]{2,0,1:T(8,128)(2,1)S(1)} %multiply_convert_fusion.2), channel_id=1, replica_groups=mesh['groups'=2,'blk'=4,'cells'=2,'rep'=2] {'blk'}, dimensions={2}, use_global_device_ids=true | all-gather | bytes 81920 | tf_op jit(solution)/shard_map/all_gather | solution.py:51
  22.9 0.0 copy-start.2
  22.9 0.0 copy-start.3
  22.9 0.0 copy-start.1
  22.9 6.9 %fusion.2 = f32[16,6,384]{2,0,1:T(8,128)} fusion(bf16[6,384,1,2048]{3,1,2,0:T(8,128)(2,1)} %param.12, bf16[16,1,2048]{2,0,1:T(8,128)(2,1)S(1)} %all_gather.3), kind=kOutput, calls=%fused_computation.2 | convolution fusion | flops 150994944 | bytes 9650176 | tf_op jit(solution)/shard_map/msc,qc->qms/dot_general | solution.py:60
  29.9 0.0 all-reduce.2.cloned.1.call-update
  29.9 0.0 copy-start
  29.9 0.0 reduce-scatter.2.cloned.1.call-start
  30.0 0.0 copy-done.2
  30.0 3.4 %collective-permute-start = (s32[256]{0:T(256)S(1)}, s32[256]{0:T(256)S(1)}, u32[]{:S(2)}, u32[]{:S(2)}) collective-permute-start(s32[256]{0:T(256)S(1)} %bitcast.33), channel_id=1, source_target_pairs={{0,2},{1,3},{4,6},{5,7},{8,10},{9,11},{12,14},{13,15},{16,18},{17,... | collective-permute-start | bytes 3080 | tf_op jit(solution)/shard_map/ppermute | solution.py:10
  33.4 0.5 fusion.15
  33.9 0.0 copy-done.3
  33.9 0.5 fusion.17
  35.0 0.0 collective-permute-done
  35.1 0.5 fusion.18
  35.5 1.3 %collective-permute-start.1 = (bf16[16,256]{1,0:T(8,128)(2,1)S(1)}, bf16[16,256]{1,0:T(8,128)(2,1)S(1)}, u32[]{:S(2)}, u32[]{:S(2)}) collective-permute-start(bf16[16,256]{1,0:T(8,128)(2,1)S(1)} %fusion.18), channel_id=1, source_target_pairs={{2,0},{3,1},{6,4},{7,5},{10,8},{11,9},{14,12},{15,13},{18,16},{19,... | collective-permute-start | bytes 24584 | tf_op jit(solution)/shard_map/ppermute | solution.py:10
  36.8 0.0 copy-done.1
  36.9 4.2 %collective-permute-done.1 = bf16[16,256]{1,0:T(8,128)(2,1)S(1)} collective-permute-done((bf16[16,256]{1,0:T(8,128)(2,1)S(1)}, bf16[16,256]{1,0:T(8,128)(2,1)S(1)}, u32[]{:S(2)}, u32[]{:S(2)}) %collective-permute-start.1) | collective-permute-done | bytes 8224 | tf_op jit(solution)/shard_map/ppermute | solution.py:10
  41.1 0.5 fusion.16
  41.6 0.5 convolution_add_fusion.2
  42.1 1.6 %collective-permute-start.2 = (f32[16,256]{1,0:T(8,128)S(1)}, f32[16,256]{1,0:T(8,128)S(1)}, u32[]{:S(2)}, u32[]{:S(2)}) collective-permute-start(f32[16,256]{1,0:T(8,128)S(1)} %get-tuple-element.5), channel_id=1, source_target_pairs={{0,2},{1,3},{4,6},{5,7},{8,10},{9,11},{12,14},{13,15},{16,18},{17,... | collective-permute-start | bytes 49160 | tf_op jit(solution)/shard_map/ppermute | solution.py:10
  43.7 0.5 fusion.14
  44.2 0.9 %collective-permute-done.2 = f32[16,256]{1,0:T(8,128)S(1)} collective-permute-done((f32[16,256]{1,0:T(8,128)S(1)}, f32[16,256]{1,0:T(8,128)S(1)}, u32[]{:S(2)}, u32[]{:S(2)}) %collective-permute-start.2) | collective-permute-done | bytes 16416 | tf_op jit(solution)/shard_map/ppermute | solution.py:10
  45.2 0.5 fusion.12
  45.7 7.2 %all-reduce.2.cloned.1.call-done = f32[16,6,384]{2,0,1:T(8,128)} async-done(((f32[16,6,384]{2,0,1:T(8,128)}), f32[16,6,384]{2,0,1:T(8,128)}) %all-reduce.2.cloned.1.call-update) | async-done | bytes 147472 | tf_op jit(solution)/shard_map/psum | solution.py:63
  52.9 0.0 copy-done
  52.9 5.1 %fusion.4 = f32[16,2048]{1,0:T(8,128)S(1)} fusion(bf16[6,384,1,2048]{3,1,2,0:T(8,128)(2,1)} %param.12, f32[16,6,384]{2,0,1:T(8,128)} %all-reduce.2.cloned.1.call-done, f32[6,384]{1,0:T(8,128)S(1)} %copy-done), kind=kOutput, calls=%fused_computation.4 | convolution fusion | flops 151068672 | bytes 9724928 | tf_op jit(solution)/shard_map/msc,qms->qc/dot_general | solution.py:65
  58.0 0.5 fusion.11
  58.5 1.1 %fusion.9 = f32[16,1,2048]{2,0,1:T(8,128)} fusion(f32[16,2048]{1,0:T(8,128)S(1)} %fusion.11, f32[16,2048]{1,0:T(8,128)S(1)} %fusion.12, s32[256]{0:T(256)S(1)} %broadcast_add_fusion, f32[16,256]{1,0:T(8,128)S(1)} %collective-permute-done.2), kind=kOutput, calls=%fused_computation.8 | convolution fusion | flops 17403904 | bytes 410624 | tf_op jit(solution)/shard_map/dot_general | solution.py:33
  59.6 0.0 reduce-scatter.2.cloned.1.call-update
  59.7 19.4 %reduce-scatter.2.cloned.1.call-done = f32[16,1,512]{2,0,1:T(8,128)} async-done(((f32[16,1,2048]{2,0,1:T(8,128)}), f32[16,1,512]{2,0,1:T(8,128)}) %reduce-scatter.2.cloned.1.call-update) | async-done | bytes 32784 | tf_op jit(solution)/shard_map/reduce_scatter | solution.py:81
  79.1 0.8 broadcast_multiply_fusion
  79.8 0.6 copy.11
  (4 shorter events, 0.0 us)
Async XLA Ops:
  6.5 46.4 %all-reduce.2.cloned.1.call-start = ((), (), s32[]{:S(2)}) async-start(), calls=%async_computation.1 | async-start | bytes 294912 | tf_op jit(solution)/shard_map/psum | solution.py:63
  22.9 7.0 %copy-start.2 = (s32[1,256]{1,0:T(1,128)S(1)}, s32[1,256]{1,0:T(1,128)}, u32[]{:S(2)}) copy-start(s32[1,256]{1,0:T(1,128)} %param.15) | copy-start | bytes 3076
  22.9 10.9 %copy-start.3 = (s32[1,256]{1,0:T(1,128)S(1)}, s32[1,256]{1,0:T(1,128)}, u32[]{:S(2)}) copy-start(s32[1,256]{1,0:T(1,128)} %param.14) | copy-start | bytes 3076
  22.9 13.9 %copy-start.1 = (f32[1,256]{1,0:T(1,128)S(1)}, f32[1,256]{1,0:T(1,128)}, u32[]{:S(2)}) copy-start(f32[1,256]{1,0:T(1,128)} %param.16) | copy-start | bytes 3076
  29.9 23.0 %copy-start = (f32[6,384]{1,0:T(8,128)S(1)}, f32[6,384]{1,0:T(8,128)}, u32[]{:S(2)}) copy-start(f32[6,384]{1,0:T(8,128)} %param.13) | copy-start | bytes 27652
  29.9 49.2 %reduce-scatter.2.cloned.1.call-start = ((), (), s32[]{:S(2)}) async-start(), calls=%async_computation.2 | async-start | bytes 163840 | tf_op jit(solution)/shard_map/reduce_scatter | solution.py:81
  30.0 5.1 %collective-permute-start = (s32[256]{0:T(256)S(1)}, s32[256]{0:T(256)S(1)}, u32[]{:S(2)}, u32[]{:S(2)}) collective-permute-start(s32[256]{0:T(256)S(1)} %bitcast.33), channel_id=1, source_target_pairs={{0,2},{1,3},{4,6},{5,7},{8,10},{9,11},{12,14},{13,15},{16,18},{17,... | collective-permute-start | bytes 3080 | tf_op jit(solution)/shard_map/ppermute | solution.py:10
  35.5 5.5 %collective-permute-start.1 = (bf16[16,256]{1,0:T(8,128)(2,1)S(1)}, bf16[16,256]{1,0:T(8,128)(2,1)S(1)}, u32[]{:S(2)}, u32[]{:S(2)}) collective-permute-start(bf16[16,256]{1,0:T(8,128)(2,1)S(1)} %fusion.18), channel_id=1, source_target_pairs={{2,0},{3,1},{6,4},{7,5},{10,8},{11,9},{14,12},{15,13},{18,16},{19,... | collective-permute-start | bytes 24584 | tf_op jit(solution)/shard_map/ppermute | solution.py:10
  42.1 3.1 %collective-permute-start.2 = (f32[16,256]{1,0:T(8,128)S(1)}, f32[16,256]{1,0:T(8,128)S(1)}, u32[]{:S(2)}, u32[]{:S(2)}) collective-permute-start(f32[16,256]{1,0:T(8,128)S(1)} %get-tuple-element.5), channel_id=1, source_target_pairs={{0,2},{1,3},{4,6},{5,7},{8,10},{9,11},{12,14},{13,15},{16,18},{17,... | collective-permute-start | bytes 49160 | tf_op jit(solution)/shard_map/ppermute | solution.py:10
Sparse Core Ops, SparseCore 0:
  30.0 22.8 all-reduce.1
  59.8 19.2 reduce-scatter.1
where the time goes:
time: 87.7 us; the launch traced here: 87.3 us
  waiting for transfers between devices  31.8 us (36%)
  matrix products  17.1 us (19%)
  blocking collectives  14.9 us (17%)
  between operations  14.1 us (16%)
  starting transfers between devices  6.36 us (7%)
  other arithmetic  2.29 us (3%)
    reduce_scatter x1, waiting for transfers between devices, on_device(): lax.psum_scatter(total_term, 'blk', scatter_dimension=2, tiled=True)  19.4 us
    all_gather x1, blocking collectives, on_device(): probe_block = lax.all_gather(weighted, 'blk', axis=2, tiled=True)  14.9 us
    psum x1, waiting for transfers between devices, on_device(): predicted = lax.psum(partial_value, 'cells')  7.25 us
    dot_general x1, matrix products, on_device(): jnp.einsum('msc,qc->qms', matrix, probe_cols, preferred_element_type=jnp....  6.94 us
    ppermute x3, starting transfers between devices, shifted(): return lax.ppermute(block, axis, route)  6.32 us
    ppermute x3, waiting for transfers between devices, shifted(): return lax.ppermute(block, axis, route)  5.15 us
    dot_general x1, matrix products, on_device(): jnp.einsum('msc,qms->qc', matrix, residual, preferred_element_type=jnp.fl...  5.1 us
    dot_general x3, matrix products, spread_flux(): jnp.dot(upper, hot, preferred_element_type=jnp.float32)  2.14 us
  transfers between devices with their start and end apart: 5, of which 4 were waited for; matrix products, arithmetic and copies ran while one was open for 4% of the time, Pallas kernels for 0%

commit v1 on v0

--- a/solution.py
+++ b/solution.py
@@ -2,6 +2,24 @@
 import jax.numpy as jnp
 from jax import lax
 from jax.sharding import PartitionSpec as P
+
+
+def joined_along(tiles, dim):
+    shape = list(tiles.shape[1:])
+    shape[dim] *= tiles.shape[0]
+    return jnp.moveaxis(tiles, 0, dim).reshape(shape)
+
+
+def collected_by_bits(value, axis):
+    size = lax.axis_size(axis)
+    pieces = value[None]
+    for level in range(size.bit_length() - 1):
+        apart = 1 << level
+        other = lax.ppermute(pieces, axis, [(i, i ^ apart) for i in range(size)])
+        both = jnp.stack([pieces, other])
+        upper = lax.axis_index(axis) >> level & 1
+        pieces = jnp.where(upper == 0, both, both[::-1]).reshape(-1, *value.shape)
+    return pieces
 
 
 def shifted(block, axis, distance):
@@ -48,7 +66,7 @@
 ):
     own_scale = level_scale(depth_level, depth_scale)
     weighted = (probes.astype(jnp.float32) * own_scale[None]).astype(jnp.bfloat16)
-    probe_block = lax.all_gather(weighted, "blk", axis=2, tiled=True)
+    probe_block = joined_along(collected_by_bits(weighted, "blk"), 2)
     slot_count = face_first.shape[1]
     live_all = (jnp.arange(slot_count, dtype=jnp.int32) < face_count[0, 0]).astype(jnp.float32)
     matrix = sensitivity[:, :, 0, :]

time: 87.7 us -> 84.6 us (0.965)
  blocking collectives: 14.9 us -> 0 us
  starting transfers between devices: 6.36 us -> 12 us
  waiting for transfers between devices: 31.8 us -> 36.4 us
  other arithmetic: 2.29 us -> 3.71 us
    all_gather x1 -> x0, blocking collectives: 14.9 us -> none  [on_device(): probe_block = lax.all_gather(weighted, 'blk', axis=2, tiled=True)]
    ppermute x0 -> x2, starting transfers between devices: none -> 5.68 us  [collected_by_bits(): other = lax.ppermute(pieces, axis, [(i, i ^ apart) for i in range(size)])]
    psum x1, waiting for transfers between devices: 7.25 us -> 9.88 us  [on_device(): predicted = lax.psum(partial_value, 'cells')]
    ppermute x0 -> x2, waiting for transfers between devices: none -> 2.46 us  [collected_by_bits(): other = lax.ppermute(pieces, axis, [(i, i ^ apart) for i in range(size)])]
  transfers between devices with their start and end apart: 5 -> 7, of which waited for: 4 -> 5; matrix products, arithmetic and copies ran while one was open for 4% -> 6% of each run, Pallas kernels for 0% -> 0%
where the time goes in v1:
time: 84.6 us; the launch traced here: 84.2 us
  waiting for transfers between devices  36.4 us (43%)
  matrix products  17.1 us (20%)
  between operations  14.2 us (17%)
  starting transfers between devices  12 us (14%)
  other arithmetic  3.71 us (4%)
    reduce_scatter x1, waiting for transfers between devices, on_device(): lax.psum_scatter(total_term, 'blk', scatter_dimension=2, tiled=True)  19.3 us
    psum x1, waiting for transfers between devices, on_device(): predicted = lax.psum(partial_value, 'cells')  9.88 us
    dot_general x1, matrix products, on_device(): jnp.einsum('msc,qc->qms', matrix, probe_cols, preferred_element_type=jnp....  6.91 us
    ppermute x3, starting transfers between devices, shifted(): return lax.ppermute(block, axis, route)  6.27 us
    ppermute x2, starting transfers between devices, collected_by_bits(): other = lax.ppermute(pieces, axis, [(i, i ^ apart) for i in range(size)])  5.68 us
    dot_general x1, matrix products, on_device(): jnp.einsum('msc,qms->qc', matrix, residual, preferred_element_type=jnp.fl...  5.1 us
    ppermute x3, waiting for transfers between devices, shifted(): return lax.ppermute(block, axis, route)  4.73 us
    ppermute x2, waiting for transfers between devices, collected_by_bits(): other = lax.ppermute(pieces, axis, [(i, i ^ apart) for i in range(size)])  2.46 us
  transfers between devices with their start and end apart: 7, of which 5 were waited for; matrix products, arithmetic and copies ran while one was open for 6% of the time, Pallas kernels for 0%

profile of v1, /device:TPU:0, one launch (start us, length us, event | category | flops | bytes accessed | tf_op | source)
XLA Modules:
  0.0 84.2 jit_solution(9420574787956643600)
XLA Ops:
  6.5 0.0 all-reduce.2.cloned.1.call-start
  6.5 0.8 select_reduce_fusion
  7.3 0.7 fusion.32
  8.0 3.0 %collective-permute-start = (bf16[1,16,1,512]{3,1,2,0:T(8,128)(2,1)S(1)}, bf16[1,16,1,512]{3,1,2,0:T(8,128)(2,1)S(1)}, u32[]{:S(2)}, u32[]{:S(2)}) collective-permute-start(bf16[1,16,1,512]{3,1,2,0:T(8,128)(2,1)S(1)} %get-tuple-element.12), channel_id=1, source_target_pairs={{0,4},{4,0},{8,12},{12,8},{1,5},{5,1},{9,13},{13,9},{2,6},{6,2},{1... | collective-permute-start | bytes 49160 | tf_op jit(solution)/shard_map/ppermute | solution.py:18
  11.1 3.4 %collective-permute-start.2 = (s32[256]{0:T(256)}, s32[256]{0:T(256)S(1)}, u32[]{:S(2)}, u32[]{:S(2)}) collective-permute-start(s32[256]{0:T(256)} %bitcast.54), channel_id=1, source_target_pairs={{0,2},{1,3},{4,6},{5,7},{8,10},{9,11},{12,14},{13,15},{16,18},{17,... | collective-permute-start | bytes 3080 | tf_op jit(solution)/shard_map/ppermute | solution.py:28
  14.5 0.7 compare_convert_fusion
  15.8 0.7 compare_select_fusion
  16.5 0.0 collective-permute-done
  16.5 2.7 %collective-permute-start.1 = (bf16[2,16,1,512]{3,1,0,2:T(8,128)(2,1)S(1)}, bf16[2,16,1,512]{3,1,0,2:T(8,128)(2,1)S(1)}, u32[]{:S(2)}, u32[]{:S(2)}) collective-permute-start(bf16[2,16,1,512]{3,1,0,2:T(8,128)(2,1)S(1)} %get-tuple-element.10), channel_id=1, source_target_pairs={{0,8},{4,12},{8,0},{12,4},{1,9},{5,13},{9,1},{13,5},{2,10},{6,14},... | collective-permute-start | bytes 98312 | tf_op jit(solution)/shard_map/ppermute | solution.py:18
  19.2 0.0 collective-permute-done.2
  19.2 2.5 %collective-permute-done.1 = bf16[2,16,1,512]{3,1,0,2:T(8,128)(2,1)S(1)} collective-permute-done((bf16[2,16,1,512]{3,1,0,2:T(8,128)(2,1)S(1)}, bf16[2,16,1,512]{3,1,0,2:T(8,128)(2,1)S(1)}, u32[]{:S(2)}, u32[]{:S(2)}) %collective-permute-start.1) | collective-permute-done | bytes 32800 | tf_op jit(solution)/shard_map/ppermute | solution.py:18
  21.7 0.1 copy.18
  21.8 0.0 copy-start.2
  21.8 0.0 copy-start.3
  21.8 6.9 %fusion.2 = f32[16,6,384]{2,0,1:T(8,128)} fusion(bf16[16,2048,1]{1,0,2:T(8,128)(2,1)S(1)} %reshape.93, bf16[6,384,1,2048]{3,1,2,0:T(8,128)(2,1)} %param.12), kind=kOutput, calls=%fused_computation.2 | convolution fusion | flops 150994944 | bytes 9650176 | tf_op jit(solution)/shard_map/msc,qc->qms/dot_general | solution.py:78
  28.7 0.0 copy-start.1
  28.7 0.0 all-reduce.2.cloned.1.call-update
  28.7 0.0 reduce-scatter.2.cloned.1.call-start
  28.8 0.0 copy-start
  28.8 0.0 copy-done.2
  28.8 0.5 fusion.15
  29.3 0.5 fusion.18
  29.8 1.3 %collective-permute-start.3 = (bf16[16,256]{1,0:T(8,128)(2,1)S(1)}, bf16[16,256]{1,0:T(8,128)(2,1)S(1)}, u32[]{:S(2)}, u32[]{:S(2)}) collective-permute-start(bf16[16,256]{1,0:T(8,128)(2,1)S(1)} %fusion.18), channel_id=1, source_target_pairs={{2,0},{3,1},{6,4},{7,5},{10,8},{11,9},{14,12},{15,13},{18,16},{19,... | collective-permute-start | bytes 24584 | tf_op jit(solution)/shard_map/ppermute | solution.py:28
  31.1 0.0 copy-done.3
  31.1 0.5 fusion.17
  31.6 3.8 %collective-permute-done.3 = bf16[16,256]{1,0:T(8,128)(2,1)S(1)} collective-permute-done((bf16[16,256]{1,0:T(8,128)(2,1)S(1)}, bf16[16,256]{1,0:T(8,128)(2,1)S(1)}, u32[]{:S(2)}, u32[]{:S(2)}) %collective-permute-start.3) | collective-permute-done | bytes 8224 | tf_op jit(solution)/shard_map/ppermute | solution.py:28
  35.4 0.0 copy-done.1
  35.4 0.5 fusion.16
  35.9 0.5 convolution_add_fusion.2
  36.4 1.6 %collective-permute-start.4 = (f32[16,256]{1,0:T(8,128)S(1)}, f32[16,256]{1,0:T(8,128)S(1)}, u32[]{:S(2)}, u32[]{:S(2)}) collective-permute-start(f32[16,256]{1,0:T(8,128)S(1)} %get-tuple-element.5), channel_id=1, source_target_pairs={{0,2},{1,3},{4,6},{5,7},{8,10},{9,11},{12,14},{13,15},{16,18},{17,... | collective-permute-start | bytes 49160 | tf_op jit(solution)/shard_map/ppermute | solution.py:28
  38.0 0.5 fusion.14
  38.5 0.9 %collective-permute-done.4 = f32[16,256]{1,0:T(8,128)S(1)} collective-permute-done((f32[16,256]{1,0:T(8,128)S(1)}, f32[16,256]{1,0:T(8,128)S(1)}, u32[]{:S(2)}, u32[]{:S(2)}) %collective-permute-start.4) | collective-permute-done | bytes 16416 | tf_op jit(solution)/shard_map/ppermute | solution.py:28
  39.4 0.5 fusion.12
  39.9 9.9 %all-reduce.2.cloned.1.call-done = f32[16,6,384]{2,0,1:T(8,128)} async-done(((f32[16,6,384]{2,0,1:T(8,128)}), f32[16,6,384]{2,0,1:T(8,128)}) %all-reduce.2.cloned.1.call-update) | async-done | bytes 147472 | tf_op jit(solution)/shard_map/psum | solution.py:81
  49.8 0.0 copy-done
  49.8 5.1 %fusion.4 = f32[16,2048]{1,0:T(8,128)S(1)} fusion(bf16[6,384,1,2048]{3,1,2,0:T(8,128)(2,1)} %param.12, f32[16,6,384]{2,0,1:T(8,128)} %all-reduce.2.cloned.1.call-done, f32[6,384]{1,0:T(8,128)S(1)} %copy-done), kind=kOutput, calls=%fused_computation.4 | convolution fusion | flops 151068672 | bytes 9724928 | tf_op jit(solution)/shard_map/msc,qms->qc/dot_general | solution.py:83
  54.9 0.5 fusion.11
  55.4 1.1 %fusion.9 = f32[16,1,2048]{2,0,1:T(8,128)} fusion(f32[16,2048]{1,0:T(8,128)S(1)} %fusion.11, f32[16,2048]{1,0:T(8,128)S(1)} %fusion.12, s32[256]{0:T(256)S(1)} %broadcast_add_fusion, f32[16,256]{1,0:T(8,128)S(1)} %collective-permute-done.4), kind=kOutput, calls=%fused_computation.8 | convolution fusion | flops 17403904 | bytes 410624 | tf_op jit(solution)/shard_map/dot_general | solution.py:51
  56.6 0.0 reduce-scatter.2.cloned.1.call-update
  56.6 19.3 %reduce-scatter.2.cloned.1.call-done = f32[16,1,512]{2,0,1:T(8,128)} async-done(((f32[16,1,2048]{2,0,1:T(8,128)}), f32[16,1,512]{2,0,1:T(8,128)}) %reduce-scatter.2.cloned.1.call-update) | async-done | bytes 32784 | tf_op jit(solution)/shard_map/reduce_scatter | solution.py:99
  75.9 0.8 broadcast_multiply_fusion
  76.7 0.6 copy.14
  (8 shorter events, 0.1 us)
Async XLA Ops:
  6.5 43.3 %all-reduce.2.cloned.1.call-start = ((), (), s32[]{:S(2)}) async-start(), calls=%async_computation.1 | async-start | bytes 294912 | tf_op jit(solution)/shard_map/psum | solution.py:81
  8.0 8.5 %collective-permute-start = (bf16[1,16,1,512]{3,1,2,0:T(8,128)(2,1)S(1)}, bf16[1,16,1,512]{3,1,2,0:T(8,128)(2,1)S(1)}, u32[]{:S(2)}, u32[]{:S(2)}) collective-permute-start(bf16[1,16,1,512]{3,1,2,0:T(8,128)(2,1)S(1)} %get-tuple-element.12), channel_id=1, source_target_pairs={{0,4},{4,0},{8,12},{12,8},{1,5},{5,1},{9,13},{13,9},{2,6},{6,2},{1... | collective-permute-start | bytes 49160 | tf_op jit(solution)/shard_map/ppermute | solution.py:18
  11.1 8.1 %collective-permute-start.2 = (s32[256]{0:T(256)}, s32[256]{0:T(256)S(1)}, u32[]{:S(2)}, u32[]{:S(2)}) collective-permute-start(s32[256]{0:T(256)} %bitcast.54), channel_id=1, source_target_pairs={{0,2},{1,3},{4,6},{5,7},{8,10},{9,11},{12,14},{13,15},{16,18},{17,... | collective-permute-start | bytes 3080 | tf_op jit(solution)/shard_map/ppermute | solution.py:28
  16.5 5.1 %collective-permute-start.1 = (bf16[2,16,1,512]{3,1,0,2:T(8,128)(2,1)S(1)}, bf16[2,16,1,512]{3,1,0,2:T(8,128)(2,1)S(1)}, u32[]{:S(2)}, u32[]{:S(2)}) collective-permute-start(bf16[2,16,1,512]{3,1,0,2:T(8,128)(2,1)S(1)} %get-tuple-element.10), channel_id=1, source_target_pairs={{0,8},{4,12},{8,0},{12,4},{1,9},{5,13},{9,1},{13,5},{2,10},{6,14},... | collective-permute-start | bytes 98312 | tf_op jit(solution)/shard_map/ppermute | solution.py:18
  21.8 7.0 %copy-start.2 = (s32[1,256]{1,0:T(1,128)S(1)}, s32[1,256]{1,0:T(1,128)}, u32[]{:S(2)}) copy-start(s32[1,256]{1,0:T(1,128)} %param.15) | copy-start | bytes 3076
  21.8 9.3 %copy-start.3 = (s32[1,256]{1,0:T(1,128)S(1)}, s32[1,256]{1,0:T(1,128)}, u32[]{:S(2)}) copy-start(s32[1,256]{1,0:T(1,128)} %param.14) | copy-start | bytes 3076
  28.7 6.7 %copy-start.1 = (f32[1,256]{1,0:T(1,128)S(1)}, f32[1,256]{1,0:T(1,128)}, u32[]{:S(2)}) copy-start(f32[1,256]{1,0:T(1,128)} %param.16) | copy-start | bytes 3076
  28.7 47.2 %reduce-scatter.2.cloned.1.call-start = ((), (), s32[]{:S(2)}) async-start(), calls=%async_computation.2 | async-start | bytes 163840 | tf_op jit(solution)/shard_map/reduce_scatter | solution.py:99
  28.8 21.0 %copy-start = (f32[6,384]{1,0:T(8,128)S(1)}, f32[6,384]{1,0:T(8,128)}, u32[]{:S(2)}) copy-start(f32[6,384]{1,0:T(8,128)} %param.13) | copy-start | bytes 27652
  29.8 5.6 %collective-permute-start.3 = (bf16[16,256]{1,0:T(8,128)(2,1)S(1)}, bf16[16,256]{1,0:T(8,128)(2,1)S(1)}, u32[]{:S(2)}, u32[]{:S(2)}) collective-permute-start(bf16[16,256]{1,0:T(8,128)(2,1)S(1)} %fusion.18), channel_id=1, source_target_pairs={{2,0},{3,1},{6,4},{7,5},{10,8},{11,9},{14,12},{15,13},{18,16},{19,... | collective-permute-start | bytes 24584 | tf_op jit(solution)/shard_map/ppermute | solution.py:28
  36.4 3.0 %collective-permute-start.4 = (f32[16,256]{1,0:T(8,128)S(1)}, f32[16,256]{1,0:T(8,128)S(1)}, u32[]{:S(2)}, u32[]{:S(2)}) collective-permute-start(f32[16,256]{1,0:T(8,128)S(1)} %get-tuple-element.5), channel_id=1, source_target_pairs={{0,2},{1,3},{4,6},{5,7},{8,10},{9,11},{12,14},{13,15},{16,18},{17,... | collective-permute-start | bytes 49160 | tf_op jit(solution)/shard_map/ppermute | solution.py:28
Sparse Core Ops, SparseCore 0:
  28.9 20.9 all-reduce.1
  56.7 19.1 reduce-scatter.1
